TPU v7x, 256 devices: a whole 4x4x8 slice. The times are simulated.
256 devices in a mesh: grp: 16 (over y, x), sq: 16 (over z, core).
Axes of the slice: x: 4, y: 4, z: 8, core: 2. Of those that a mesh axis runs over, the one named last changes fastest.
Arguments:
- queries: bfloat16 [65536, 4096], P(('grp', 'sq')), parts along dimension 0, may hold values from -6 to 6
- keys: bfloat16 [65536, 1024], P(('grp', 'sq')), parts along dimension 0, may hold values from -6 to 6
- values: bfloat16 [65536, 1024], P(('grp', 'sq')), parts along dimension 0, may hold values from -6 to 6
- tile_lists: int32 [512, 32, 16], P('grp'), parts along dimension 0, may hold values from 0 to 31, as said below
- tile_counts: int32 [512, 32], P('grp'), parts along dimension 0, may hold values from 1 to 16, as said below
Outputs:
- attended: bfloat16 [65536, 4096], P(('grp', 'sq')), parts along dimension 0
There are 16 independent parts, one for each index of `grp`. A program takes and returns all parts, laid end to end along the dimension named above; each array names one. Nothing has to cross between parts.
Inputs may be any that keep to these rules, and one draw needn't show every extreme that they name: tile_counts[h, b] = min(b + 1, c_h) with a cap c_h for each head h; at least one head has cap 16. tile_lists[h, b, j] for j < tile_counts[h, b] are distinct key blocks from 0 to b, the first one being b; the later entries equal b.
All inputs are finite; a program needn't handle non-finite values.
Results may differ from a plain program's by a relative error of at most 0.0042.
Values may be sent and summed in bfloat16 or wider, within the bound.
A program may use at most 64 MiB of HBM per device.

v0:
```python
import jax
import jax.numpy as jnp
from jax import lax
from jax.sharding import PartitionSpec as P

HEAD_DIM = 128
TILE = 128


def attend_head(query_head, key_head, value_head, lists, counts, query_blocks):
    width = query_head.shape[1]
    tiles_here = query_head.shape[0] // TILE
    blocks = key_head.shape[0] // TILE
    query_tiles = query_head.reshape(tiles_here, TILE, width)
    key_tiles = key_head.reshape(blocks, TILE, width)
    value_tiles = value_head.reshape(blocks, TILE, width)
    scaling = width ** (-0.5)
    offsets = jnp.arange(TILE, dtype=jnp.int32)
    query_position = query_blocks[:, None] * TILE + offsets[None, :]

    def advance(tile_turn, state_now):
        run_max, run_sum, running = state_now
        chosen = lax.dynamic_index_in_dim(lists, tile_turn, axis=1, keepdims=False)
        is_live = tile_turn < counts
        key_block = jnp.take(key_tiles, chosen, axis=0)
        value_block = jnp.take(value_tiles, chosen, axis=0)
        scores = (
            jnp.einsum("bid,bjd->bij", query_tiles, key_block, preferred_element_type=jnp.float32)
            * scaling
        )
        key_position = chosen[:, None] * TILE + offsets[None, :]
        allowed = (key_position[:, None, :] <= query_position[:, :, None]) & is_live[:, None, None]
        masked = jnp.where(allowed, scores, jnp.float32(-1e30))
        new_max = jnp.maximum(run_max, jnp.max(masked, axis=2))
        weights = jnp.where(allowed, jnp.exp(masked - new_max[:, :, None]), jnp.float32(0.0))
        factor = jnp.exp(run_max - new_max)
        run_sum = run_sum * factor + jnp.sum(weights, axis=2)
        running = running * factor[:, :, None] + jnp.einsum(
            "bij,bjd->bid",
            weights.astype(jnp.bfloat16),
            value_block,
            preferred_element_type=jnp.float32,
        )
        return (new_max, run_sum, running)

    initial = (
        jnp.full((tiles_here, TILE), -1e30, jnp.float32),
        jnp.zeros((tiles_here, TILE), jnp.float32),
        jnp.zeros((tiles_here, TILE, width), jnp.float32),
    )
    run_max, run_sum, running = lax.fori_loop(jnp.int32(0), jnp.max(counts), advance, initial)
    return (running / run_sum[:, :, None]).astype(jnp.bfloat16).reshape(tiles_here * TILE, width)


def body(queries, keys, values, tile_lists, tile_counts):
    tok_rows = queries.shape[0]
    head_count = tile_counts.shape[0]
    block_total = tile_counts.shape[1]
    kv_count = keys.shape[1] // HEAD_DIM
    devices = lax.axis_size("sq")
    per_device = head_count // devices
    query_heads = queries.reshape(tok_rows, head_count, HEAD_DIM)
    key_heads = keys.reshape(tok_rows, kv_count, HEAD_DIM)
    value_heads = values.reshape(tok_rows, kv_count, HEAD_DIM)
    my_index = lax.axis_index("sq")
    all_blocks = jnp.arange(block_total, dtype=jnp.int32)
    outputs = []
    copies = max(1, devices // kv_count)
    received = (
        lax.all_to_all(query_heads, "sq", split_axis=1, concat_axis=0, tiled=True),
        lax.all_to_all(
            jnp.repeat(key_heads, copies, axis=1), "sq", split_axis=1, concat_axis=0, tiled=True
        ),
        lax.all_to_all(
            jnp.repeat(value_heads, copies, axis=1), "sq", split_axis=1, concat_axis=0, tiled=True
        ),
    )
    my_heads = my_index * per_device + jnp.arange(per_device, dtype=jnp.int32)
    kv_share = max(1, kv_count // devices)
    kv_position = [position // (per_device // kv_share) for position in range(per_device)]
    query_mine, key_mine, value_mine = received
    for position in range(per_device):
        head_id = my_heads[position]
        outputs.append(
            attend_head(
                query_mine[:, position],
                key_mine[:, kv_position[position]],
                value_mine[:, kv_position[position]],
                tile_lists[head_id],
                tile_counts[head_id],
                all_blocks,
            )
        )
    stacked = jnp.stack(outputs, axis=1)
    returned = lax.all_to_all(stacked, "sq", split_axis=0, concat_axis=1, tiled=True)
    return returned.reshape(tok_rows, head_count * HEAD_DIM)


def solution(mesh):
    placed = (
        P(("grp", "sq"), None),
        P(("grp", "sq"), None),
        P(("grp", "sq"), None),
        P("grp", None, None),
        P("grp", None),
    )
    return jax.shard_map(
        body, mesh=mesh, in_specs=placed, out_specs=P(("grp", "sq"), None), check_vma=False
    )
```

profile of v0, /device:TPU:7, one launch (start us, length us, event | category | flops | bytes accessed | tf_op | source)
XLA Modules:
  0.0 672.3 jit_solution(11233885394073636810)
XLA Ops:
  2.3 9.2 %all-to-all-start.2 = ((bf16[256,16,128]{2,0,1:T(8,128)(2,1)}), bf16[256,16,128]{2,0,1:T(8,128)(2,1)}, u32[]{:S(2)}, u32[]{:S(2)}) async-start(bf16[256,16,128]{2,0,1:T(8,128)(2,1)} %bitcast.12), calls=%async_computation.2 | async-start | bytes 2097152 | tf_op jit(solution)/shard_map/all_to_all | solution.py:74
  11.5 3.3 copy.43
  17.6 21.9 %all-to-all-done.2 = bf16[256,16,128]{2,0,1:T(8,128)(2,1)} async-done(((bf16[256,16,128]{2,0,1:T(8,128)(2,1)}), bf16[256,16,128]{2,0,1:T(8,128)(2,1)}, u32[]{:S(2)}, u32[]{:S(2)}) %all-to-all-start.2) | async-done | bytes 1048608 | tf_op jit(solution)/shard_map/all_to_all | solution.py:74
  39.5 3.6 all-to-all-start.1
  44.3 47.7 %all-to-all-done.1 = bf16[256,32,128]{2,0,1:T(8,128)(2,1)S(1)} async-done(((bf16[256,32,128]{2,0,1:T(8,128)(2,1)}), bf16[256,32,128]{2,0,1:T(8,128)(2,1)S(1)}, u32[]{:S(2)}, u32[]{:S(2)}) %all-to-all-start.1) | async-done | bytes 2097184 | tf_op jit(solution)/shard_map/all_to_all | solution.py:70
  93.2 5.0 all-to-all-start
  106.3 19.9 %all-to-all-done = bf16[256,16,128]{2,0,1:T(8,128)(2,1)} async-done(((bf16[256,16,128]{2,0,1:T(8,128)(2,1)}), bf16[256,16,128]{2,0,1:T(8,128)(2,1)}, u32[]{:S(2)}, u32[]{:S(2)}) %all-to-all-start) | async-done | bytes 1048608 | tf_op jit(solution)/shard_map/all_to_all | solution.py:71
  127.7 72.2 %while.30 = (s32[]{:T(128)}, f32[32,128]{1,0:T(8,128)S(1)}, f32[32,128]{1,0:T(8,128)S(1)}, f32[32,128,128]{2,1,0:T(8,128)}, s32[]{:T(128)}, /*index=5*/s32[32,16...) while((s32[]{:T(128)}, f32[32,128]{1,0:T(8,128)S(1)}, ...), condition=%wide.region_4.6_spmd.clone, body=%wide.region_1.5_spmd.clone.sunk | while | flops 278414592 | bytes 18224788 | solution.py:51
  137.6 4.5 multiply_add_fusion.9
  151.9 4.5 multiply_add_fusion.9
  166.2 4.5 multiply_add_fusion.9
  180.5 4.5 multiply_add_fusion.9
  194.9 4.5 multiply_add_fusion.9
  201.5 43.9 %while.31 = (s32[]{:T(128)}, f32[32,128]{1,0:T(8,128)S(1)}, f32[32,128]{1,0:T(8,128)S(1)}, f32[32,128,128]{2,1,0:T(8,128)}, s32[]{:T(128)}, /*index=5*/s32[32,16...) while((s32[]{:T(128)}, f32[32,128]{1,0:T(8,128)S(1)}, ...), condition=%wide.region_9.11_spmd.clone, body=%wide.region_6.10_spmd.clone.sunk | while | flops 278414592 | bytes 18224788 | solution.py:51
  202.3 2.9 gather_fusion.2
  208.6 2.9 gather_fusion.3
  211.5 4.4 multiply_add_fusion.11
  216.7 2.9 gather_fusion.2
  223.0 2.9 gather_fusion.3
  225.9 4.4 multiply_add_fusion.11
  240.3 4.4 multiply_add_fusion.11
  248.6 17.8 %copy.47 = bf16[4096,2,128]{2,1,0:T(2,128)(2,1)S(1)} copy(bf16[4096,2,128]{2,0,1:T(8,128)(2,1)S(1)} %pad_maximum_fusion) | data formatting | bytes 4194304 | tf_op jit(solution)/shard_map/stack | solution.py:94
  266.4 398.9 %all_to_all.63 = bf16[4096,2,128]{2,1,0:T(2,128)(2,1)S(1)} all-to-all(bf16[4096,2,128]{2,1,0:T(2,128)(2,1)S(1)} %copy.47), channel_id=1, replica_groups=mesh['grp'=16,'sq'=16] {'sq'}, dimensions={0} | all-to-all | bytes 4194304 | tf_op jit(solution)/shard_map/all_to_all | solution.py:95
  668.2 4.1 copy.50
  (111 shorter events, 82.7 us)
Async XLA Ops:
  0.0 1.0 copy-start
  2.3 37.2 %all-to-all-start.2 = ((bf16[256,16,128]{2,0,1:T(8,128)(2,1)}), bf16[256,16,128]{2,0,1:T(8,128)(2,1)}, u32[]{:S(2)}, u32[]{:S(2)}) async-start(bf16[256,16,128]{2,0,1:T(8,128)(2,1)} %bitcast.12), calls=%async_computation.2 | async-start | bytes 2097152 | tf_op jit(solution)/shard_map/all_to_all | solution.py:74
  39.5 52.5 %all-to-all-start.1 = ((bf16[256,32,128]{2,0,1:T(8,128)(2,1)}), bf16[256,32,128]{2,0,1:T(8,128)(2,1)S(1)}, u32[]{:S(2)}, u32[]{:S(2)}) async-start(bf16[256,32,128]{2,0,1:T(8,128)(2,1)} %copy.44), calls=%async_computation.1 | async-start | bytes 4194304 | tf_op jit(solution)/shard_map/all_to_all | solution.py:70
  93.2 33.0 %all-to-all-start = ((bf16[256,16,128]{2,0,1:T(8,128)(2,1)}), bf16[256,16,128]{2,0,1:T(8,128)(2,1)}, u32[]{:S(2)}, u32[]{:S(2)}) async-start(bf16[256,16,128]{2,0,1:T(8,128)(2,1)} %bitcast.74), calls=%async_computation | async-start | bytes 2097152 | tf_op jit(solution)/shard_map/all_to_all | solution.py:71
  245.5 2.2 copy-start.1
where the time goes:
time: 677 us; the launch traced here: 672 us
  blocking collectives  399 us (59%)
  waiting for transfers between devices  89.5 us (13%)
  local copies, waits for them, and re-layouts  87.9 us (13%)
  matrix products  54.6 us (8%)
  starting transfers between devices  17.7 us (3%)
  other arithmetic  12.7 us (2%)
  loops' own time  7.12 us (1%)
    all_to_all x1, blocking collectives, body(): lax.all_to_all(stacked, 'sq', split_axis=0, concat_axis=1, tiled=True)  399 us
    all_to_all x1, waiting for transfers between devices, body(): lax.all_to_all(query_heads, 'sq', split_axis=1, concat_axis=0, tiled=True)  47.7 us
    dot_general x8, matrix products, advance(): jnp.einsum('bij,bjd->bid', weights.astype(jnp.bfloat16), value_block, pre...  35.6 us
    gather x8, local copies, waits for them, and re-layouts, advance(): value_block = jnp.take(value_tiles, chosen, axis=0)  23.1 us
    gather x8, local copies, waits for them, and re-layouts, advance(): key_block = jnp.take(key_tiles, chosen, axis=0)  23.1 us
    all_to_all x1, waiting for transfers between devices, body(): lax.all_to_all(jnp.repeat(value_heads, copies, axis=1), 'sq', split_axis=...  21.9 us
    all_to_all x1, waiting for transfers between devices, body(): lax.all_to_all(jnp.repeat(key_heads, copies, axis=1), 'sq', split_axis=1,...  19.9 us
    dot_general x8, matrix products, advance(): jnp.einsum('bid,bjd->bij', query_tiles, key_block, preferred_element_type...  19 us
  transfers between devices with their start and end apart: 3, of which 3 were waited for; matrix products, arithmetic and copies ran while one was open for 2% of the time, Pallas kernels for 0%

commit v1 on v0

v1 whole, which is shorter than its diff:
```python
import functools

import jax
import jax.numpy as jnp
from jax import lax
from jax.experimental import pallas as pl
from jax.experimental.pallas import tpu as pltpu
from jax.sharding import PartitionSpec as P

MESH = pl.DeviceIdType.MESH
HEAD_DIM = 128
TILE = 128
CHIPS = 8
LAG = 2
LOW = -1e30
LOG2E = 1.4426950408889634

DO_COMM = True
DO_COMPUTE = True


def kernel(kv_count, group, tiles, q_ref, k_ref, v_ref, lists_ref, counts_ref, out_ref, *scratch):
    kv = scratch[:kv_count]
    q_t, scores, recv, plus_sem, minus_sem, twin_sem = scratch[kv_count:]
    rank = lax.axis_index("sq")
    z, core = rank // 2, rank % 2
    right = lax.rem(z + 1, CHIPS) * 2 + core
    left = lax.rem(z + CHIPS - 1, CHIPS) * 2 + core
    twin = z * 2 + (1 - core)

    barrier = pltpu.get_barrier_semaphore()
    for other in (left, right, twin):
        pl.semaphore_signal(barrier, inc=1, device_id={"sq": other}, device_id_type=MESH)

    for h in range(kv_count):
        cols = pl.ds(h * HEAD_DIM, HEAD_DIM)
        for half in range(2):
            rows = pl.ds(half * TILE, TILE)
            kv[h][rank * 2 + half, 0] = k_ref[rows, cols]
            kv[h][rank * 2 + half, 1] = v_ref[rows, cols].T
    pl.semaphore_wait(barrier, 3)

    def piece(h, source, sem, target):
        at = kv[h].at[pl.ds(source * 2, 2)]
        return pltpu.make_async_remote_copy(
            src_ref=at,
            dst_ref=at,
            send_sem=sem,
            recv_sem=recv.at[h, source],
            device_id={"sq": target},
            device_id_type=MESH,
        )

    def goes_up(h, j):
        source = z - j
        near = (source >= 0) & (z < CHIPS - 1)
        if j < 3:
            return near, source
        return near & (source == 3) & (h % 2 == 0), source

    def goes_down(h, j):
        source = lax.rem(z + j, CHIPS)
        return source <= (2 if h % 2 == 0 else 3), source

    def from_below(h, j):
        source = z - j
        if j < 4:
            return source >= 0, source
        return (source == 3) & (h % 2 == 0), source

    def from_above(h, j):
        source = lax.rem(z + j, CHIPS)
        return source <= (2 if h % 2 == 0 else 3), source

    def up(h, j, source):
        return piece(h, source * 2 + core, plus_sem.at[h, j], right)

    def down(h, j, source):
        return piece(h, source * 2 + core, minus_sem.at[h, j], left)

    def across(h, source):
        return piece(h, source * 2 + core, twin_sem.at[h, source], twin)

    def own(h):
        for go, make in ((goes_up, up), (goes_down, down)):
            cond, source = go(h, 0)

            @pl.when(cond)
            def _():
                make(h, 0, source).start()

        across(h, z).start()

    def arrive(h, j):
        for come, go, make in ((from_below, goes_up, up), (from_above, goes_down, down)):
            cond, source = come(h, j)

            @pl.when(cond)
            def _():
                piece(h, source * 2 + core, plus_sem.at[h, 0], right).wait_recv()
                if j < 4:
                    more, _ = go(h, j)

                    @pl.when(more)
                    def _():
                        make(h, j, source).start()

                @pl.when(source < z)
                def _():
                    across(h, source).start()

    def settle(h):
        def one(source, carry):
            piece(h, source * 2 + 1 - core, plus_sem.at[h, 0], right).wait_recv()
            return carry

        lax.fori_loop(0, z + 1, one, 0)

    def sent(h):
        for j in range(4):
            for go, make in ((goes_up, up), (goes_down, down)):
                cond, source = go(h, j)

                @pl.when(cond)
                def _():
                    make(h, j, source).wait_send()

        def one(source, carry):
            across(h, source).wait_send()
            return carry

        lax.fori_loop(0, z + 1, one, 0)

    key_at = lax.broadcasted_iota(jnp.int32, (TILE, TILE), 0)
    query_at = lax.broadcasted_iota(jnp.int32, (TILE, TILE), 1)
    causal = key_at <= query_at
    factor = (HEAD_DIM ** -0.5) * LOG2E

    def attend(h, unit):
        head = h * group + unit // 2
        half = unit % 2
        block = rank * 2 + half
        count = counts_ref[head, block]
        turned = q_t[head * 2 + half]
        best = jnp.full((8, TILE), LOW, jnp.float32)
        for j in range(tiles):
            at = lists_ref[head, block, j]
            s = jnp.dot(kv[h][at, 0], turned, preferred_element_type=jnp.float32)
            if j == 0:
                s = jnp.where(causal, s, LOW)
            scores[j] = s
            top = jnp.max(s.reshape(TILE // 8, 8, TILE), axis=0)
            best = jnp.maximum(best, jnp.where(j < count, top, LOW))
        best = jnp.max(best, axis=0, keepdims=True) * factor
        total = jnp.zeros((8, TILE), jnp.float32)
        result = jnp.zeros((HEAD_DIM, TILE), jnp.float32)
        for j in range(tiles):
            at = lists_ref[head, block, j]
            floor = jnp.where(j < count, best, 1e30)
            weights = jnp.exp2(scores[j] * factor - floor)
            total = total + jnp.sum(weights.reshape(TILE // 8, 8, TILE), axis=0)
            result = result + jnp.dot(
                kv[h][at, 1], weights.astype(jnp.bfloat16), preferred_element_type=jnp.float32
            )
        total = jnp.sum(total, axis=0, keepdims=True)
        done = (result * (1.0 / total)).T.astype(jnp.bfloat16)
        out_ref[
            pl.ds(pl.multiple_of(half * TILE, TILE), TILE),
            pl.ds(pl.multiple_of(head * HEAD_DIM, HEAD_DIM), HEAD_DIM),
        ] = done

    def turn(head, carry):
        for half in range(2):
            cols = pl.ds(pl.multiple_of(head * HEAD_DIM, HEAD_DIM), HEAD_DIM)
            q_t[head * 2 + half] = q_ref[pl.ds(half * TILE, TILE), cols].T
        return carry

    last = kv_count - 1 + 4 * LAG
    for t in range(last + 1):
        if DO_COMM:
            if t < kv_count:
                own(t)
            for j in range(1, 5):
                h = t - LAG * j
                if 0 <= h < kv_count:
                    arrive(h, j)
        if t == 0:
            lax.fori_loop(0, kv_count * group, turn, 0)
        h = t - 4 * LAG
        if 0 <= h < kv_count:
            if DO_COMM:
                settle(h)
            if DO_COMPUTE:

                def step(unit, carry):
                    attend(h, unit)
                    return carry

                lax.fori_loop(0, group * 2, step, 0)
    if DO_COMM:
        for h in range(kv_count):
            sent(h)


def body(queries, keys, values, tile_lists, tile_counts):
    rows, width = queries.shape
    kv_count = keys.shape[1] // HEAD_DIM
    heads, blocks, tiles = tile_lists.shape
    group = heads // kv_count
    ranks = lax.axis_size("sq")
    vmem = pl.BlockSpec(memory_space=pltpu.VMEM)
    smem = pl.BlockSpec(memory_space=pltpu.SMEM)
    return pl.pallas_call(
        functools.partial(kernel, kv_count, group, tiles),
        out_shape=jax.ShapeDtypeStruct((rows, width), jnp.bfloat16),
        in_specs=[vmem, vmem, vmem, smem, smem],
        out_specs=vmem,
        scratch_shapes=[pltpu.VMEM((blocks, 2, TILE, HEAD_DIM), jnp.bfloat16)] * kv_count
        + [
            pltpu.VMEM((heads * 2, HEAD_DIM, TILE), jnp.bfloat16),
            pltpu.VMEM((tiles, TILE, TILE), jnp.float32),
            pltpu.SemaphoreType.DMA((kv_count, ranks)),
            pltpu.SemaphoreType.DMA((kv_count, 4)),
            pltpu.SemaphoreType.DMA((kv_count, 4)),
            pltpu.SemaphoreType.DMA((kv_count, ranks // 2)),
        ],
        compiler_params=pltpu.CompilerParams(
            collective_id=0, has_side_effects=True, vmem_limit_bytes=48 * 1024 * 1024
        ),
    )(queries, keys, values, tile_lists, tile_counts)


def solution(mesh):
    placed = (
        P(("grp", "sq"), None),
        P(("grp", "sq"), None),
        P(("grp", "sq"), None),
        P("grp", None, None),
        P("grp", None),
    )
    return jax.shard_map(
        body, mesh=mesh, in_specs=placed, out_specs=P(("grp", "sq"), None), check_vma=False
    )
```

time: 677 us -> 139 us (0.21)
  the two profiles are of different devices: /device:TPU:7 before, /device:TPU:229 now
where the time goes in v1:
time: 139 us
  Pallas kernels  132 us (95%)
  local copies, waits for them, and re-layouts  6.87 us (5%)
    pallas_call x1, Pallas kernels, body(): pl.pallas_call(functools.partial(kernel, kv_count, group, tiles), out_sha...  132 us
    unnamed x10, local copies, waits for them, and re-layouts  6.87 us

profile of v1, /device:TPU:229, one launch (start us, length us, event | category | flops | bytes accessed | tf_op | source)
XLA Modules:
  0.0 139.0 jit_solution(6184786008965285804)
XLA Ops:
  0.0 1.2 copy.6.lists_ref
  1.2 0.0 copy-start
  1.2 1.6 %copy-done = bf16[256,4096]{1,0:T(8,128)(2,1)S(1)} copy-done((bf16[256,4096]{1,0:T(8,128)(2,1)S(1)}, bf16[256,4096]{1,0:T(8,128)(2,1)}, u32[]{:S(2)}) %copy-start) | copy-done | bytes 2097176
  2.8 0.0 copy-start.1
  2.8 1.0 copy-done.1
  3.8 0.0 copy-start.2
  3.8 1.0 copy-done.2
  4.9 0.0 copy-start.3
  4.9 0.7 copy-done.3
  5.6 132.1 %shard_map.55 = bf16[256,4096]{1,0:T(8,128)(2,1)S(1)} custom-call(bf16[256,4096]{1,0:T(8,128)(2,1)S(1)} %copy-done, bf16[256,1024]{1,0:T(8,128)(2,1)S(1)} %copy-done.1, bf16[256,1024]{1,0:T(8,128)(2,1)S(1)} %copy-done.2, s32[32,32,16]{2,1,0:T(8,128)S(1)} %copy.6.lists_ref, s32[32,32]{1,0:T(8,128)S(1)} %copy-done.3), custom_call_target="tpu_custom_call" | custom-call | tf_op jit(solution)/shard_map/pallas_call | solution.py:213
  137.7 1.3 copy.8
Async XLA Ops:
  1.2 1.6 %copy-start = (bf16[256,4096]{1,0:T(8,128)(2,1)S(1)}, bf16[256,4096]{1,0:T(8,128)(2,1)}, u32[]{:S(2)}) copy-start(bf16[256,4096]{1,0:T(8,128)(2,1)} %q_ref.1) | copy-start | bytes 6291460
  2.8 1.0 copy-start.1
  3.8 1.0 copy-start.2
  4.9 0.7 copy-start.3

commit v2 on v1

--- a/solution.py
+++ b/solution.py
@@ -11,7 +11,8 @@
 HEAD_DIM = 128
 TILE = 128
 CHIPS = 8
-LAG = 2
+LAG = 1
+JOINT = 4
 LOW = -1e30
 LOG2E = 1.4426950408889634
 
@@ -19,9 +20,25 @@
 DO_COMPUTE = True
 
 
-def kernel(kv_count, group, tiles, q_ref, k_ref, v_ref, lists_ref, counts_ref, out_ref, *scratch):
+def kernel(kv_count, group, tiles, q_hbm, k_hbm, v_hbm, lists_hbm, counts_hbm, out_ref, *scratch):
     kv = scratch[:kv_count]
-    q_t, scores, recv, plus_sem, minus_sem, twin_sem = scratch[kv_count:]
+    q_ref, k_ref, v_ref, lists_ref, counts_ref, q_t = scratch[kv_count : kv_count + 6]
+    wide_a, wide_b, scores_a, scores_b, best_a, best_b = scratch[kv_count + 6 : kv_count + 12]
+    load, recv, plus_sem, minus_sem, twin_sem = scratch[kv_count + 12 :]
+    loads = [
+        pltpu.make_async_copy(src, dst, load.at[i])
+        for i, (src, dst) in enumerate(
+            (
+                (k_hbm, k_ref),
+                (v_hbm, v_ref),
+                (q_hbm, q_ref),
+                (lists_hbm, lists_ref),
+                (counts_hbm, counts_ref),
+            )
+        )
+    ]
+    for copy in loads:
+        copy.start()
     rank = lax.axis_index("sq")
     z, core = rank // 2, rank % 2
     right = lax.rem(z + 1, CHIPS) * 2 + core
@@ -32,6 +49,10 @@
     for other in (left, right, twin):
         pl.semaphore_signal(barrier, inc=1, device_id={"sq": other}, device_id_type=MESH)
 
+    wide_a[...] = jnp.zeros_like(wide_a)
+    wide_b[...] = jnp.zeros_like(wide_b)
+    loads[0].wait()
+    loads[1].wait()
     for h in range(kv_count):
         cols = pl.ds(h * HEAD_DIM, HEAD_DIM)
         for half in range(2):
@@ -131,43 +152,86 @@
 
         lax.fori_loop(0, z + 1, one, 0)
 
-    key_at = lax.broadcasted_iota(jnp.int32, (TILE, TILE), 0)
-    query_at = lax.broadcasted_iota(jnp.int32, (TILE, TILE), 1)
+    key_at = lax.broadcasted_iota(jnp.int32, (TILE, 2 * TILE), 0)
+    query_at = lax.rem(lax.broadcasted_iota(jnp.int32, (TILE, 2 * TILE), 1), TILE)
     causal = key_at <= query_at
-    factor = (HEAD_DIM ** -0.5) * LOG2E
-
-    def attend(h, unit):
-        head = h * group + unit // 2
-        half = unit % 2
-        block = rank * 2 + half
-        count = counts_ref[head, block]
-        turned = q_t[head * 2 + half]
-        best = jnp.full((8, TILE), LOW, jnp.float32)
+    factor = (HEAD_DIM**-0.5) * LOG2E
+
+    def pair(first, second):
+        return jnp.concatenate([first, second], axis=1)
+
+    def side(x, half):
+        return x[:, half * TILE : (half + 1) * TILE]
+
+    def listed(head, half, j):
+        return lists_ref[head, j, rank * 2 + half]
+
+    def live(head, j, x, other):
+        return pair(
+            *[
+                jnp.where(j < counts_ref[head, rank * 2 + half], side(x, half), other)
+                for half in range(2)
+            ]
+        )
+
+    def score(h, head, wide, scores, best_ref):
+        for half in range(2):
+            at = pl.ds(half * TILE, TILE)
+            wide[at, at] = q_t[head * 2 + half]
+        listed_keys = [
+            pair(*[kv[h][listed(head, half, j), 0] for half in range(2)]) for j in range(tiles)
+        ]
+        all_scores = jnp.dot(
+            jnp.concatenate(listed_keys, axis=0), wide[...], preferred_element_type=jnp.float32
+        )
+        best = jnp.full((8, 2 * TILE), LOW, jnp.float32)
         for j in range(tiles):
-            at = lists_ref[head, block, j]
-            s = jnp.dot(kv[h][at, 0], turned, preferred_element_type=jnp.float32)
+            s = all_scores[j * TILE : (j + 1) * TILE]
             if j == 0:
                 s = jnp.where(causal, s, LOW)
             scores[j] = s
-            top = jnp.max(s.reshape(TILE // 8, 8, TILE), axis=0)
-            best = jnp.maximum(best, jnp.where(j < count, top, LOW))
-        best = jnp.max(best, axis=0, keepdims=True) * factor
-        total = jnp.zeros((8, TILE), jnp.float32)
-        result = jnp.zeros((HEAD_DIM, TILE), jnp.float32)
-        for j in range(tiles):
-            at = lists_ref[head, block, j]
-            floor = jnp.where(j < count, best, 1e30)
-            weights = jnp.exp2(scores[j] * factor - floor)
-            total = total + jnp.sum(weights.reshape(TILE // 8, 8, TILE), axis=0)
-            result = result + jnp.dot(
-                kv[h][at, 1], weights.astype(jnp.bfloat16), preferred_element_type=jnp.float32
-            )
-        total = jnp.sum(total, axis=0, keepdims=True)
-        done = (result * (1.0 / total)).T.astype(jnp.bfloat16)
-        out_ref[
-            pl.ds(pl.multiple_of(half * TILE, TILE), TILE),
-            pl.ds(pl.multiple_of(head * HEAD_DIM, HEAD_DIM), HEAD_DIM),
-        ] = done
+            top = jnp.max(s.reshape(TILE // 8, 8, 2 * TILE), axis=0)
+            best = jnp.maximum(best, live(head, j, top, LOW))
+        best_ref[...] = best
+
+    def attend(h, head, scores, best_ref):
+        best = jnp.max(best_ref[...], axis=0, keepdims=True) * factor
+        total = jnp.zeros((8, 2 * TILE), jnp.float32)
+        result = [jnp.zeros((HEAD_DIM, TILE), jnp.float32)] * 2
+        for first in range(0, tiles, JOINT):
+            weights = []
+            for j in range(first, first + JOINT):
+                w = jnp.exp2(scores[j] * factor - live(head, j, best, 1e30))
+                total = total + jnp.sum(w.reshape(TILE // 8, 8, 2 * TILE), axis=0)
+                weights.append(w.astype(jnp.bfloat16))
+            weights = jnp.concatenate(weights, axis=0)
+            for half in range(2):
+                turned = [kv[h][listed(head, half, j), 1] for j in range(first, first + JOINT)]
+                result[half] = result[half] + jnp.dot(
+                    jnp.concatenate(turned, axis=1),
+                    side(weights, half),
+                    preferred_element_type=jnp.float32,
+                )
+        scale = 1.0 / jnp.sum(total, axis=0, keepdims=True)
+        for half in range(2):
+            out_ref[
+                pl.ds(half * TILE, TILE),
+                pl.ds(pl.multiple_of(head * HEAD_DIM, HEAD_DIM), HEAD_DIM),
+            ] = (result[half] * side(scale, half)).T.astype(jnp.bfloat16)
+
+    def attend_group(h):
+        first = h * group
+        score(h, first, wide_a, scores_a, best_a)
+
+        def step(i, carry):
+            head = first + 2 * i
+            score(h, head + 1, wide_b, scores_b, best_b)
+            attend(h, head, scores_a, best_a)
+            score(h, jnp.minimum(head + 2, first + group - 1), wide_a, scores_a, best_a)
+            attend(h, head + 1, scores_b, best_b)
+            return carry
+
+        lax.fori_loop(0, group // 2, step, 0)
 
     def turn(head, carry):
         for half in range(2):
@@ -185,18 +249,15 @@
                 if 0 <= h < kv_count:
                     arrive(h, j)
         if t == 0:
+            for copy in loads[2:]:
+                copy.wait()
             lax.fori_loop(0, kv_count * group, turn, 0)
         h = t - 4 * LAG
         if 0 <= h < kv_count:
             if DO_COMM:
                 settle(h)
             if DO_COMPUTE:
-
-                def step(unit, carry):
-                    attend(h, unit)
-                    return carry
-
-                lax.fori_loop(0, group * 2, step, 0)
+                attend_group(h)
     if DO_COMM:
         for h in range(kv_count):
             sent(h)
@@ -208,26 +269,39 @@
     heads, blocks, tiles = tile_lists.shape
     group = heads // kv_count
     ranks = lax.axis_size("sq")
-    vmem = pl.BlockSpec(memory_space=pltpu.VMEM)
-    smem = pl.BlockSpec(memory_space=pltpu.SMEM)
+    any_place = pl.BlockSpec(memory_space=pl.ANY)
+    scores = pltpu.VMEM((tiles, TILE, 2 * TILE), jnp.float32)
+    wide = pltpu.VMEM((2 * TILE, 2 * TILE), jnp.bfloat16)
+    best = pltpu.VMEM((8, 2 * TILE), jnp.float32)
     return pl.pallas_call(
         functools.partial(kernel, kv_count, group, tiles),
         out_shape=jax.ShapeDtypeStruct((rows, width), jnp.bfloat16),
-        in_specs=[vmem, vmem, vmem, smem, smem],
-        out_specs=vmem,
+        in_specs=[any_place] * 5,
+        out_specs=pl.BlockSpec(memory_space=pltpu.VMEM),
         scratch_shapes=[pltpu.VMEM((blocks, 2, TILE, HEAD_DIM), jnp.bfloat16)] * kv_count
         + [
+            pltpu.VMEM(queries.shape, jnp.bfloat16),
+            pltpu.VMEM(keys.shape, jnp.bfloat16),
+            pltpu.VMEM(values.shape, jnp.bfloat16),
+            pltpu.SMEM((heads, tiles, blocks), jnp.int32),
+            pltpu.SMEM(tile_counts.shape, jnp.int32),
             pltpu.VMEM((heads * 2, HEAD_DIM, TILE), jnp.bfloat16),
-            pltpu.VMEM((tiles, TILE, TILE), jnp.float32),
+            wide,
+            wide,
+            scores,
+            scores,
+            best,
+            best,
+            pltpu.SemaphoreType.DMA((5,)),
             pltpu.SemaphoreType.DMA((kv_count, ranks)),
             pltpu.SemaphoreType.DMA((kv_count, 4)),
             pltpu.SemaphoreType.DMA((kv_count, 4)),
             pltpu.SemaphoreType.DMA((kv_count, ranks // 2)),
         ],
         compiler_params=pltpu.CompilerParams(
-            collective_id=0, has_side_effects=True, vmem_limit_bytes=48 * 1024 * 1024
+            collective_id=0, has_side_effects=True, vmem_limit_bytes=60 * 1024 * 1024
         ),
-    )(queries, keys, values, tile_lists, tile_counts)
+    )(queries, keys, values, jnp.swapaxes(tile_lists, 1, 2), tile_counts)
 
 
 def solution(mesh):

time: 139 us -> 103 us (0.74)
  Pallas kernels: 132 us -> 99.9 us
  local copies, waits for them, and re-layouts: 6.87 us -> 3.13 us
    pallas_call x1, Pallas kernels: 132 us -> 99.9 us  [body(): pl.pallas_call(functools.partial(kernel, kv_count, group, tiles), out_sha...]
    unnamed x10 -> x1, local copies, waits for them, and re-layouts: 6.87 us -> 3.13 us
where the time goes in v2:
time: 103 us
  Pallas kernels  99.9 us (97%)
  local copies, waits for them, and re-layouts  3.13 us (3%)
    pallas_call x1, Pallas kernels, body(): pl.pallas_call(functools.partial(kernel, kv_count, group, tiles), out_sha...  99.9 us
    unnamed x1, local copies, waits for them, and re-layouts  3.13 us

profile of v2, /device:TPU:229, one launch (start us, length us, event | category | flops | bytes accessed | tf_op | source)
XLA Modules:
  0.0 103.1 jit_solution(1290678438286767854)
XLA Ops:
  0.0 99.9 %shard_map.55 = bf16[256,4096]{1,0:T(8,128)(2,1)} custom-call(bf16[256,4096]{1,0:T(8,128)(2,1)} %q_hbm.1, bf16[256,1024]{1,0:T(8,128)(2,1)} %k_hbm.1, bf16[256,1024]{1,0:T(8,128)(2,1)} %v_hbm.1, s32[32,16,32]{2,1,0:T(8,128)} %bitcast.1, s32[32,32]{1,0:T(8,128)} %counts_hbm.1), custom_call_target="tpu_custom_call" | custom-call | tf_op jit(solution)/shard_map/pallas_call | solution.py:276
  100.0 3.1 %copy.7 = bf16[256,4096]{1,0:T(8,128)(2,1)} copy(bf16[256,4096]{1,0:T(8,128)(2,1)} %shard_map.55) | data formatting | bytes 4194304

commit v3 on v2

v3 whole, which is shorter than its diff:
```python
import functools
import heapq

import jax
import jax.numpy as jnp
from jax import lax
from jax.experimental import pallas as pl
from jax.experimental.pallas import tpu as pltpu
from jax.sharding import PartitionSpec as P

MESH = pl.DeviceIdType.MESH
HEAD_DIM = 128
TILE = 128
CHIPS = 8
JOINT = 4
LOW = -1e30
LOG2E = 1.4426950408889634

DO_COMM = True
DO_COMPUTE = True

PIECE, HOP, WORK, BEGIN, AHEAD, FAR = 2.8, 3.0, 3.8, 1.0, 3.0, 1.5


def plain(first, third, fourth):
    route = {0: first, 1: (3, 4), 2: third, 3: fourth}
    return {}, route | {source: (7, None) for source in (4, 5, 6)}


PLAN = (
    plain((3, 4), (4, 5), (7, None)),
    plain((2, 3), (4, 5), (7, None)),
    ({7: 6}, {source: (6, None) for source in range(6)} | {7: (None, 6)}),
    plain((4, 5), (4, 5), (7, None)),
    (
        {6: 5, 7: 0},
        {0: (5, None)}
        | {source: (5, 0) for source in (1, 2, 3, 4)}
        | {5: (None, 0), 6: (0, 5), 7: (0, None)},
    ),
    plain((4, 5), (4, 5), (5, 6)),
    plain((3, 4), (5, 6), (5, 6)),
    plain((4, 5), (6, 7), (5, 6)),
)
AWAY = tuple((h, chip, site) for h, (away, _) in enumerate(PLAN) for chip, site in away.items())


def walk(first, last, step):
    path = [first]
    while path[-1] != last:
        path.append((path[-1] + step) % CHIPS)
    return path


def needed(h, chip):
    away = PLAN[h][0]
    if chip in away:
        return 0
    return 1 + max([chip] + [other for other, site in away.items() if site == chip])


def reckon(ready):
    events, count, waiting, busy, arrive, sends = [], 0, {}, set(), {}, []

    def put(time, what):
        nonlocal count
        heapq.heappush(events, (time, count, what))
        count += 1

    for h, (away, route) in enumerate(PLAN):
        for source, ends in route.items():
            for end, step in zip(ends, (1, -1)):
                if end is not None:
                    put(BEGIN, (("kv", h, source), 1, step, walk(source, end, step), 0))
        for chip, site in away.items():
            step = 1 if (site - chip) % CHIPS == 1 else -1
            put(BEGIN + 5.0, (("q", h, chip), 2, step, [chip, site], 0))
            put(ready.get((h, chip), 1e6), (("o", h, chip), 2, -step, [site, chip], 0))
    while events:
        now, _, what = heapq.heappop(events)
        if len(what) == 2:
            link = what
            busy.discard(link)
        else:
            name, size, step, path, at = what
            if at:
                arrive[name, path[at]] = now
            if at == len(path) - 1:
                continue
            link = (step, path[at])
            rank = name[1] - (3 if name[0] != "kv" else 0) - FAR * (len(path) - 1 - at)
            waiting.setdefault(link, []).append((rank, count, what))
        if waiting.get(link) and link not in busy:
            waiting[link].sort()
            name, size, step, path, at = waiting[link].pop(0)[2]
            busy.add(link)
            sends.append((now, name, step, path[at]))
            put(now + size * PIECE, link)
            put(now + size * PIECE + HOP, (name, size, step, path, at + 1))
    return arrive, sends


def schedule():
    ready = {}
    for _ in range(4):
        arrive, sends = reckon(ready)
        full = [max(t for (n, _), t in arrive.items() if n[:2] == ("kv", h)) for h in range(len(PLAN))]
        steps = [(full[h], h, None, None) for h in range(len(PLAN))]
        for h, chip, site in AWAY:
            steps.append((max(full[h], arrive[("q", h, chip), site]) + WORK, h, chip, site))
        steps.sort(key=lambda step: step[0])
        begin = [[] for _ in range(CHIPS)]
        ready = {}
        for chip in range(CHIPS):
            now = 0.0
            for t, h, away, site in steps:
                takes = chip not in PLAN[h][0] if site is None else chip == site
                now = max(now, full[h] if site is None else arrive[("q", h, away), site])
                begin[chip].append((now, takes))
                now += WORK if takes else 0.0
                if takes and site is not None:
                    ready[h, away] = now + 0.5
    work = []
    for chip in range(CHIPS):
        actions = []
        for (name, at), t in arrive.items():
            if at == chip and name[0] != "o":
                actions.append((t, 0, len(actions), ("take", name, 0)))
        for t, name, step, at in sends:
            if at == chip and name[0] != "o":
                here = arrive.get((name, chip), BEGIN + (5.0 if name[0] == "q" else 0.0))
                actions.append((max(here, t - AHEAD), 1, len(actions), ("send", name, step)))
        for h in range(len(PLAN)):
            if needed(h, chip):
                actions.append((BEGIN + 4.0 * h, 2, len(actions), ("give", ("kv", h, chip), 0)))
        actions.sort()
        ends = [BEGIN + 1.0]
        for t, takes in begin[chip]:
            ends += [t + 0.01, t + WORK / 2 if takes else 0.0]
        parts = []
        for end in ends + [1e9]:
            parts.append([action[3] for action in actions if action[0] < end])
            actions = [action for action in actions if action[0] >= end]
        work.append(parts)
    return [step[1:3] for step in steps], work, max(
        [t + WORK * takes for times in begin for t, takes in times] + [t for (n, _), t in arrive.items() if n[0] == "o"]
    )


def kernel(kv_count, group, tiles, q_hbm, k_hbm, v_hbm, lists_hbm, counts_hbm, out_ref, *scratch):
    kv = scratch[:kv_count]
    q_ref, k_ref, v_ref, lists_ref, counts_ref, q_t = scratch[kv_count : kv_count + 6]
    wide_a, wide_b, scores_a, scores_b, best_a, best_b = scratch[kv_count + 6 : kv_count + 12]
    away_q, away_out = scratch[kv_count + 12 : kv_count + 14]
    load, recv, up_sem, down_sem, twin_sem, away_send, away_recv = scratch[kv_count + 14 :]
    loads = [
        pltpu.make_async_copy(src, dst, load.at[i])
        for i, (src, dst) in enumerate(
            (
                (k_hbm, k_ref),
                (v_hbm, v_ref),
                (q_hbm, q_ref),
                (lists_hbm, lists_ref),
                (counts_hbm, counts_ref),
            )
        )
    ]
    for copy in loads:
        copy.start()
    rank = lax.axis_index("sq")
    z, core = rank // 2, rank % 2
    right = lax.rem(z + 1, CHIPS) * 2 + core
    left = lax.rem(z + CHIPS - 1, CHIPS) * 2 + core
    twin = z * 2 + (1 - core)

    barrier = pltpu.get_barrier_semaphore()
    for other in (left, right, twin):
        pl.semaphore_signal(barrier, inc=1, device_id={"sq": other}, device_id_type=MESH)

    wide_a[...] = jnp.zeros_like(wide_a)
    wide_b[...] = jnp.zeros_like(wide_b)
    loads[0].wait()
    loads[1].wait()
    for h in range(kv_count):
        cols = pl.ds(h * HEAD_DIM, HEAD_DIM)
        for half in range(2):
            rows = pl.ds(half * TILE, TILE)
            kv[h][rank * 2 + half, 0] = k_ref[rows, cols]
            kv[h][rank * 2 + half, 1] = v_ref[rows, cols].T
    pl.semaphore_wait(barrier, 3)

    def piece(h, source, sem, target):
        at = kv[h].at[pl.ds(source * 2, 2)]
        return pltpu.make_async_remote_copy(
            src_ref=at,
            dst_ref=at,
            send_sem=sem,
            recv_sem=recv.at[h, source],
            device_id={"sq": target},
            device_id_type=MESH,
        )

    def along(h, source, step):
        sem = (up_sem if step == 1 else down_sem).at[h, source]
        return piece(h, source * 2 + core, sem, right if step == 1 else left)

    def across(h, source):
        return piece(h, source * 2 + core, twin_sem.at[h, source], twin)

    def beyond(kind, h, chip):
        e = [item[:2] for item in AWAY].index((h, chip))
        site = AWAY[e][2]
        goal = site if kind == "q" else chip
        src = q_t.at[pl.ds(h * group * 2, group * 2)] if kind == "q" else away_out.at[e]
        return pltpu.make_async_remote_copy(
            src_ref=src,
            dst_ref=away_q.at[e] if kind == "q" else away_out.at[e],
            send_sem=away_send.at[e, 0 if kind == "q" else 1],
            recv_sem=away_recv.at[e, 0 if kind == "q" else 1],
            device_id={"sq": goal * 2 + core},
            device_id_type=MESH,
        )

    def act(chip, action):
        what, (kind, h, source), step = action
        if what == "take" and kind == "q":
            beyond("q", h, source).wait_recv()
        elif what == "take":
            along(h, source, 1).wait_recv()
            if source < needed(h, chip):
                across(h, source).start()
        elif what == "give":
            across(h, source).start()
        elif kind == "q":
            beyond("q", h, source).start()
        else:
            along(h, source, step).start()

    def settle(h, chip):
        def one(source, carry):
            piece(h, source * 2 + 1 - core, twin_sem.at[h, source], twin).wait_recv()
            return carry

        lax.fori_loop(0, needed(h, chip), one, 0)

    def sent(chip):
        for part in work[chip]:
            for what, (kind, h, source), step in part:
                if what == "send" and kind == "q":
                    beyond("q", h, source).wait_send()
                elif what == "send":
                    along(h, source, step).wait_send()
        for h in range(kv_count):

            def one(source, carry):
                across(h, source).wait_send()
                return carry

            lax.fori_loop(0, needed(h, chip), one, 0)

    key_at = lax.broadcasted_iota(jnp.int32, (TILE, 2 * TILE), 0)
    query_at = lax.rem(lax.broadcasted_iota(jnp.int32, (TILE, 2 * TILE), 1), TILE)
    causal = key_at <= query_at
    factor = (HEAD_DIM**-0.5) * LOG2E

    def pair(first, second):
        return jnp.concatenate([first, second], axis=1)

    def side(x, half):
        return x[:, half * TILE : (half + 1) * TILE]

    def listed(head, owner, half, j):
        return lists_ref[head, j, owner * 2 + half]

    def live(head, owner, j, x, other):
        return pair(
            *[
                jnp.where(j < counts_ref[head, owner * 2 + half], side(x, half), other)
                for half in range(2)
            ]
        )

    def score(h, i, owner, turned, wide, scores, best_ref):
        head = h * group + i
        for half in range(2):
            at = pl.ds(half * TILE, TILE)
            wide[at, at] = turned[i * 2 + half]
        listed_keys = [
            pair(*[kv[h][listed(head, owner, half, j), 0] for half in range(2)]) for j in range(tiles)
        ]
        all_scores = jnp.dot(
            jnp.concatenate(listed_keys, axis=0), wide[...], preferred_element_type=jnp.float32
        )
        best = jnp.full((8, 2 * TILE), LOW, jnp.float32)
        for j in range(tiles):
            s = all_scores[j * TILE : (j + 1) * TILE]
            if j == 0:
                s = jnp.where(causal, s, LOW)
            scores[j] = s
            top = jnp.max(s.reshape(TILE // 8, 8, 2 * TILE), axis=0)
            best = jnp.maximum(best, live(head, owner, j, top, LOW))
        best_ref[...] = best

    def attend(h, i, owner, scores, best_ref, out):
        head = h * group + i
        best = jnp.max(best_ref[...], axis=0, keepdims=True) * factor
        total = jnp.zeros((8, 2 * TILE), jnp.float32)
        result = [jnp.zeros((HEAD_DIM, TILE), jnp.float32)] * 2
        for first in range(0, tiles, JOINT):
            weights = []
            for j in range(first, first + JOINT):
                w = jnp.exp2(scores[j] * factor - live(head, owner, j, best, 1e30))
                total = total + jnp.sum(w.reshape(TILE // 8, 8, 2 * TILE), axis=0)
                weights.append(w.astype(jnp.bfloat16))
            weights = jnp.concatenate(weights, axis=0)
            for half in range(2):
                turned = [kv[h][listed(head, owner, half, j), 1] for j in range(first, first + JOINT)]
                result[half] = result[half] + jnp.dot(
                    jnp.concatenate(turned, axis=1),
                    side(weights, half),
                    preferred_element_type=jnp.float32,
                )
        scale = 1.0 / jnp.sum(total, axis=0, keepdims=True)
        for half in range(2):
            out[
                pl.ds(half * TILE, TILE),
                pl.ds(pl.multiple_of(i * HEAD_DIM, HEAD_DIM), HEAD_DIM),
            ] = (result[half] * side(scale, half)).T.astype(jnp.bfloat16)

    steps, work, _ = schedule()

    def pass_on(number, settling, when=None):
        if not DO_COMM:
            return
        for chip in range(CHIPS):
            if not work[chip][number] and (settling is None or not needed(settling, chip)):
                continue

            @pl.when(z == chip if when is None else (z == chip) & when)
            def _():
                for action in work[chip][number]:
                    act(chip, action)
                if settling is not None:
                    settle(settling, chip)

    def attend_group(h, owner, turned, out, number):
        score(h, 0, owner, turned, wide_a, scores_a, best_a)

        def step(k, carry):
            i = 2 * k
            pass_on(number, None, k == 1)
            score(h, i + 1, owner, turned, wide_b, scores_b, best_b)
            attend(h, i, owner, scores_a, best_a, out)
            score(h, jnp.minimum(i + 2, group - 1), owner, turned, wide_a, scores_a, best_a)
            attend(h, i + 1, owner, scores_b, best_b, out)
            return carry

        lax.fori_loop(0, group // 2, step, 0)

    def turn(head, carry):
        for half in range(2):
            cols = pl.ds(pl.multiple_of(head * HEAD_DIM, HEAD_DIM), HEAD_DIM)
            q_t[head * 2 + half] = q_ref[pl.ds(half * TILE, TILE), cols].T
        return carry

    pass_on(0, None)
    for copy in loads[2:]:
        copy.wait()
    lax.fori_loop(0, kv_count * group, turn, 0)
    for number, (h, chip) in enumerate(steps):
        pass_on(2 * number + 1, h if chip is None else None)
        columns = pl.ds(h * group * HEAD_DIM, group * HEAD_DIM)
        if chip is None:
            here = z >= 0
            for other in PLAN[h][0]:
                here = here & (z != other)

            @pl.when(here)
            def _():
                if DO_COMPUTE:
                    turned = q_t.at[pl.ds(h * group * 2, group * 2)]
                    attend_group(h, rank, turned, out_ref.at[:, columns], 2 * number + 2)

        else:
            e = [item[:2] for item in AWAY].index((h, chip))

            @pl.when(z == AWAY[e][2])
            def _():
                if DO_COMPUTE:
                    attend_group(h, chip * 2 + core, away_q.at[e], away_out.at[e], 2 * number + 2)
                if DO_COMM:
                    beyond("o", h, chip).start()

    pass_on(2 * len(steps) + 1, None)
    if DO_COMM:
        for e, (h, chip, site) in enumerate(AWAY):

            @pl.when(z == chip)
            def _():
                beyond("o", h, chip).wait_recv()
                out_ref[:, pl.ds(h * group * HEAD_DIM, group * HEAD_DIM)] = away_out[e]

            @pl.when(z == site)
            def _():
                beyond("o", h, chip).wait_send()

        for chip in range(CHIPS):

            @pl.when(z == chip)
            def _():
                sent(chip)


def body(queries, keys, values, tile_lists, tile_counts):
    rows, width = queries.shape
    kv_count = keys.shape[1] // HEAD_DIM
    heads, blocks, tiles = tile_lists.shape
    group = heads // kv_count
    ranks = lax.axis_size("sq")
    hbm = pl.BlockSpec(memory_space=pltpu.HBM)
    scores = pltpu.VMEM((tiles, TILE, 2 * TILE), jnp.float32)
    wide = pltpu.VMEM((2 * TILE, 2 * TILE), jnp.bfloat16)
    best = pltpu.VMEM((8, 2 * TILE), jnp.float32)
    return pl.pallas_call(
        functools.partial(kernel, kv_count, group, tiles),
        out_shape=jax.ShapeDtypeStruct((rows, width), jnp.bfloat16),
        in_specs=[hbm] * 5,
        out_specs=pl.BlockSpec(memory_space=pltpu.VMEM),
        scratch_shapes=[pltpu.VMEM((blocks, 2, TILE, HEAD_DIM), jnp.bfloat16)] * kv_count
        + [
            pltpu.VMEM(queries.shape, jnp.bfloat16),
            pltpu.VMEM(keys.shape, jnp.bfloat16),
            pltpu.VMEM(values.shape, jnp.bfloat16),
            pltpu.SMEM((heads, tiles, blocks), jnp.int32),
            pltpu.SMEM(tile_counts.shape, jnp.int32),
            pltpu.VMEM((heads * 2, HEAD_DIM, TILE), jnp.bfloat16),
            wide,
            wide,
            scores,
            scores,
            best,
            best,
            pltpu.VMEM((len(AWAY), group * 2, HEAD_DIM, TILE), jnp.bfloat16),
            pltpu.VMEM((len(AWAY), rows, group * HEAD_DIM), jnp.bfloat16),
            pltpu.SemaphoreType.DMA((5,)),
            pltpu.SemaphoreType.DMA((kv_count, ranks)),
            pltpu.SemaphoreType.DMA((kv_count, CHIPS)),
            pltpu.SemaphoreType.DMA((kv_count, CHIPS)),
            pltpu.SemaphoreType.DMA((kv_count, CHIPS)),
            pltpu.SemaphoreType.DMA((len(AWAY), 2)),
            pltpu.SemaphoreType.DMA((len(AWAY), 2)),
        ],
        compiler_params=pltpu.CompilerParams(
            collective_id=0, has_side_effects=True, vmem_limit_bytes=34 * 1024 * 1024
        ),
    )(
        *[
            pltpu.with_memory_space_constraint(x, pltpu.HBM)
            for x in (queries, keys, values, jnp.swapaxes(tile_lists, 1, 2), tile_counts)
        ]
    )


def solution(mesh):
    placed = (
        P(("grp", "sq"), None),
        P(("grp", "sq"), None),
        P(("grp", "sq"), None),
        P("grp", None, None),
        P("grp", None),
    )
    return jax.shard_map(
        body, mesh=mesh, in_specs=placed, out_specs=P(("grp", "sq"), None), check_vma=False
    )
```

time: 103 us -> 86.8 us (0.84)
  Pallas kernels: 99.9 us -> 85 us
  local copies, waits for them, and re-layouts: 3.13 us -> 1.32 us
    pallas_call x1, Pallas kernels: 99.9 us -> 85 us  [body(): pl.pallas_call(functools.partial(kernel, kv_count, group, tiles), out_sha...]
    unnamed x1, local copies, waits for them, and re-layouts: 3.13 us -> 1.32 us
where the time goes in v3:
time: 86.8 us; the launch traced here: 86.3 us
  Pallas kernels  85 us (98%)
  local copies, waits for them, and re-layouts  1.32 us (2%)
    pallas_call x1, Pallas kernels, body(): pl.pallas_call(functools.partial(kernel, kv_count, group, tiles), out_sha...  85 us

profile of v3, /device:TPU:229, one launch (start us, length us, event | category | flops | bytes accessed | tf_op | source)
XLA Modules:
  0.0 86.3 jit_solution(8281042114103354034)
XLA Ops:
  0.0 85.0 %shard_map.55 = bf16[256,4096]{1,0:T(8,128)(2,1)S(1)} custom-call(bf16[256,4096]{1,0:T(8,128)(2,1)} %q_hbm.1, bf16[256,1024]{1,0:T(8,128)(2,1)} %k_hbm.1, bf16[256,1024]{1,0:T(8,128)(2,1)} %v_hbm.1, s32[32,16,32]{2,1,0:T(8,128)} %bitcast.1, s32[32,32]{1,0:T(8,128)} %counts_hbm.1), custom_call_target="tpu_custom_call" | custom-call | tf_op jit(solution)/shard_map/pallas_call | solution.py:424
  85.0 1.3 %copy.7 = bf16[256,4096]{1,0:T(8,128)(2,1)} copy(bf16[256,4096]{1,0:T(8,128)(2,1)S(1)} %shard_map.55) | data formatting | bytes 4194304

commit v4 on v3

--- a/solution.py
+++ b/solution.py
@@ -12,7 +12,7 @@
 HEAD_DIM = 128
 TILE = 128
 CHIPS = 8
-JOINT = 4
+JOINT = 2
 LOW = -1e30
 LOG2E = 1.4426950408889634
 
@@ -126,6 +126,8 @@
         for (name, at), t in arrive.items():
             if at == chip and name[0] != "o":
                 actions.append((t, 0, len(actions), ("take", name, 0)))
+                if name[0] == "kv" and name[2] < needed(name[1], chip):
+                    actions.append((t, 2, len(actions), ("give", name, 0)))
         for t, name, step, at in sends:
             if at == chip and name[0] != "o":
                 here = arrive.get((name, chip), BEGIN + (5.0 if name[0] == "q" else 0.0))
@@ -177,8 +179,6 @@
     for other in (left, right, twin):
         pl.semaphore_signal(barrier, inc=1, device_id={"sq": other}, device_id_type=MESH)
 
-    wide_a[...] = jnp.zeros_like(wide_a)
-    wide_b[...] = jnp.zeros_like(wide_b)
     loads[0].wait()
     loads[1].wait()
     for h in range(kv_count):
@@ -227,8 +227,6 @@
             beyond("q", h, source).wait_recv()
         elif what == "take":
             along(h, source, 1).wait_recv()
-            if source < needed(h, chip):
-                across(h, source).start()
         elif what == "give":
             across(h, source).start()
         elif kind == "q":
@@ -364,6 +362,8 @@
         return carry
 
     pass_on(0, None)
+    wide_a[...] = jnp.zeros_like(wide_a)
+    wide_b[...] = jnp.zeros_like(wide_b)
     for copy in loads[2:]:
         copy.wait()
     lax.fori_loop(0, kv_count * group, turn, 0)
@@ -377,6 +377,8 @@
 
             @pl.when(here)
             def _():
+                if not DO_COMPUTE:
+                    pass_on(2 * number + 2, None)
                 if DO_COMPUTE:
                     turned = q_t.at[pl.ds(h * group * 2, group * 2)]
                     attend_group(h, rank, turned, out_ref.at[:, columns], 2 * number + 2)
@@ -386,6 +388,8 @@
 
             @pl.when(z == AWAY[e][2])
             def _():
+                if not DO_COMPUTE:
+                    pass_on(2 * number + 2, None)
                 if DO_COMPUTE:
                     attend_group(h, chip * 2 + core, away_q.at[e], away_out.at[e], 2 * number + 2)
                 if DO_COMM:

time: 86.8 us -> 86.6 us (level)
  no operation moved by 1% of the time
where the time goes in v4:
time: 86.6 us; the launch traced here: 86.1 us
  Pallas kernels  84.8 us (98%)
  local copies, waits for them, and re-layouts  1.32 us (2%)
    pallas_call x1, Pallas kernels, body(): pl.pallas_call(functools.partial(kernel, kv_count, group, tiles), out_sha...  84.8 us

profile of v4, /device:TPU:229, one launch (start us, length us, event | category | flops | bytes accessed | tf_op | source)
XLA Modules:
  0.0 86.1 jit_solution(11785354612254247735)
XLA Ops:
  0.0 84.8 %shard_map.55 = bf16[256,4096]{1,0:T(8,128)(2,1)S(1)} custom-call(bf16[256,4096]{1,0:T(8,128)(2,1)} %q_hbm.1, bf16[256,1024]{1,0:T(8,128)(2,1)} %k_hbm.1, bf16[256,1024]{1,0:T(8,128)(2,1)} %v_hbm.1, s32[32,16,32]{2,1,0:T(8,128)} %bitcast.1, s32[32,32]{1,0:T(8,128)} %counts_hbm.1), custom_call_target="tpu_custom_call" | custom-call | tf_op jit(solution)/shard_map/pallas_call | solution.py:428
  84.8 1.3 %copy.7 = bf16[256,4096]{1,0:T(8,128)(2,1)} copy(bf16[256,4096]{1,0:T(8,128)(2,1)S(1)} %shard_map.55) | data formatting | bytes 4194304
